TPU v7x, 512 devices: a whole 4x8x8 slice. The times are simulated.
512 devices in a mesh: lat: 32 (over z_lo, x, core), chan: 16 (over z_hi, y).
Axes of the slice: x: 4, y: 8, z: 8 (z_hi: 2, z_lo: 4; z = z_hi * 4 + z_lo), core: 2. Of those that a mesh axis runs over, the one named last changes fastest.
Arguments:
- atmosphere: bfloat16 [256, 256, 1536], P('chan', 'lat'), may hold values from -6 to 6
- first_weight: bfloat16 [256, 16, 5, 5], P('chan'), may hold values from -0.3125 to 0.3125
- first_bias: float32 [256], P('chan'), may hold values from -3 to 3
- second_weight: bfloat16 [256, 16, 5, 5], P('chan'), may hold values from -0.3125 to 0.3125
Outputs:
- spectrum: float32 [128, 2, 256, 2, 128], P('lat', None, 'chan')
All inputs are finite; a program needn't handle non-finite values.
Results may differ from a plain program's by a relative error of at most 0.007.
Values may be sent and summed in bfloat16 or wider, within the bound.
A program may use at most 64 MiB of HBM per device.

v0:
```python
import math

import jax
import jax.numpy as jnp
from jax import lax
from jax.sharding import PartitionSpec as P

ORDERS = 128
DEGREES = 256


def extended_2(shard, sides, width):
    for axis, dim in sides:
        devices, length = (lax.axis_size(axis), shard.shape[dim])
        up = [(i, (i + 1) % devices) for i in range(devices - 1)]
        down = [(j, i) for i, j in up]
        last = lax.slice_in_dim(shard, length - width, length, axis=dim)
        initial = lax.slice_in_dim(shard, 0, width, axis=dim)
        before = lax.ppermute(last, axis, up)
        after = lax.ppermute(initial, axis, down)
        shard = jnp.concatenate([before, shard, after], axis=dim)
    return shard


def partner(value, axis, apart):
    mask = 2**apart
    pairs = [(source, source ^ mask) for source in range(lax.axis_size(axis))]
    return lax.ppermute(value, axis, pairs)


def fourier_table(length, orders):
    places = lax.broadcasted_iota(jnp.int32, (length, orders), 0)
    numbers = lax.broadcasted_iota(jnp.int32, (length, orders), 1) + 1
    phases = (places * numbers % length).astype(jnp.float32) * (2.0 * math.pi / length)
    factor = 1.0 / math.sqrt(length)
    return (jnp.concatenate([jnp.cos(phases), -jnp.sin(phases)], axis=1) * factor).astype(
        jnp.bfloat16
    )


def legendre(colatitude, orders, degrees):
    cosine = jnp.cos(colatitude)[None, :]
    sines = jnp.sin(colatitude)[None, :]
    order_real = orders.astype(jnp.float32)[:, None]
    log_diag = 0.5 * (
        jnp.log((2.0 * order_real + 1.0) / 2.0)
        + lax.lgamma(2.0 * order_real + 1.0)
        - order_real * math.log(4.0)
        - 2.0 * lax.lgamma(order_real + 1.0)
    ) + order_real * jnp.log(sines)
    diagonal = jnp.exp(log_diag)
    empty_rows = jnp.zeros_like(diagonal)

    def advance(carried, degree):
        latest, before = carried
        degree_real = degree.astype(jnp.float32)
        spread = jnp.maximum(degree_real * degree_real - order_real * order_real, 1.0)
        raising = jnp.sqrt(jnp.maximum(4.0 * degree_real * degree_real - 1.0, 1.0) / spread)
        previous = degree_real - 1.0
        lowering = jnp.sqrt(
            jnp.maximum(previous * previous - order_real * order_real, 0.0)
            / jnp.maximum(4.0 * previous * previous - 1.0, 1.0)
        )
        raised = raising * (cosine * latest - lowering * before)
        result = jnp.where(
            degree_real == order_real, diagonal, jnp.where(degree_real > order_real, raised, 0.0)
        )
        return ((result, latest), result)

    _, stacked = lax.scan(
        advance, (empty_rows, empty_rows), jnp.arange(degrees, dtype=jnp.int32), unroll=16
    )
    return stacked


def weighted_table(north_rows, orders, total_rows, degrees):
    colatitude = math.pi * (north_rows.astype(jnp.float32) + 0.5) / total_rows
    quadrature = math.pi * jnp.sin(colatitude) / math.sqrt(total_rows)
    return legendre(colatitude, orders, degrees) * quadrature[None, None, :]


def project(even_sum, odd_sum, stacked, orders):
    degrees, number, height = stacked.shape
    paired = (
        stacked.reshape(degrees // 2, 2, number, height).transpose(2, 1, 3, 0).astype(jnp.bfloat16)
    )
    parity = (orders[:, None] + jnp.arange(2, dtype=jnp.int32)[None, :]) % 2 == 0
    selected = jnp.where(parity, even_sum[..., None], odd_sum[..., None])
    return jnp.einsum("crakq,kqrj->kqcaj", selected, paired, preferred_element_type=jnp.float32)


def convolve(padded, kernel):
    radius = kernel.shape[3] // 2
    widened = jnp.concatenate([padded[..., -radius:], padded, padded[..., :radius]], axis=2)
    result = lax.conv_general_dilated(
        widened[None],
        kernel,
        (1, 1),
        "VALID",
        feature_group_count=padded.shape[0] // kernel.shape[1],
        preferred_element_type=jnp.float32,
    )
    return result[0]


def extend(grid_field, rim_width):
    return extended_2(grid_field, (("lat", 1),), rim_width)


def per_device(atmosphere, first_weight, first_bias, second_weight):
    members = lax.axis_size("lat")
    halfway = members // 2
    position = lax.axis_index("lat")
    southern = position >= halfway
    band_rows = atmosphere.shape[1]
    circle = atmosphere.shape[2]
    radius = first_weight.shape[3] // 2
    offsets = first_bias[:, None, None]
    extended = extend(atmosphere, radius)
    hidden = jax.nn.gelu(convolve(extended, first_weight) + offsets, approximate=False).astype(
        jnp.bfloat16
    )
    updated = atmosphere.astype(jnp.float32) + convolve(extend(hidden, radius), second_weight)
    updated = updated.astype(jnp.bfloat16)
    fourier = fourier_table(circle, ORDERS)
    spectra = jnp.dot(updated.reshape(-1, circle), fourier, preferred_element_type=jnp.float32)
    spectra = spectra.astype(jnp.bfloat16).reshape(atmosphere.shape[0], band_rows, 2, ORDERS)
    half_rows = band_rows // 2
    leading = spectra[:, :half_rows]
    incoming = spectra[:, half_rows:]
    for bit in range(members.bit_length() - 1):
        incoming = partner(incoming, "lat", bit)
    north_part = jnp.where(southern, incoming, leading).astype(jnp.float32)
    south_part = jnp.where(southern, leading[:, ::-1], incoming[:, ::-1]).astype(jnp.float32)
    even_sum = (north_part + south_part).astype(jnp.bfloat16)
    odd_sum = (north_part - south_part).astype(jnp.bfloat16)
    total_rows = band_rows * members
    band_number = jnp.where(southern, members - 1 - position, position)
    own_rows = (
        band_number * band_rows
        + jnp.where(southern, half_rows, 0)
        + jnp.arange(half_rows, dtype=jnp.int32)
    )
    all_orders = jnp.arange(1, ORDERS + 1, dtype=jnp.int32)
    spherical_all = weighted_table(own_rows, all_orders, total_rows, DEGREES)
    numbers = (
        jnp.int32(0) + 1 + jnp.arange(lax.axis_size("lat") * (ORDERS // members), dtype=jnp.int32)
    )
    return lax.psum_scatter(
        project(even_sum, odd_sum, spherical_all, numbers), "lat", scatter_dimension=0, tiled=True
    )


def solution(mesh):
    placed = (
        P("chan", "lat", None),
        P("chan", None, None, None),
        P("chan"),
        P("chan", None, None, None),
    )
    return jax.shard_map(
        per_device,
        mesh=mesh,
        in_specs=placed,
        out_specs=P("lat", None, "chan", None, None),
        check_vma=False,
    )
```

profile of v0, /device:TPU:1, one launch (start us, length us, event | category | flops | bytes accessed | tf_op | source)
XLA Modules:
  0.0 485.1 jit_solution(17018243480483220669)
XLA Ops:
  7.8 4.5 collective-permute-start
  12.4 5.6 %collective-permute-start.1 = (bf16[16,2,1536]{2,1,0:T(2,128)(2,1)S(1)}, bf16[16,2,1536]{2,1,0:T(2,128)(2,1)S(1)}, u32[]{:S(2)}, u32[]{:S(2)}) collective-permute-start(bf16[16,2,1536]{2,1,0:T(2,128)(2,1)S(1)} %get-tuple-element.666), channel_id=1, source_target_pairs={{16,0},{32,16},{48,32},{64,48},{80,64},{96,80},{112,96},{128,112},... | collective-permute-start | bytes 294920 | tf_op jit(solution)/shard_map/ppermute | solution.py:20
  18.0 4.2 fusion.62
  25.9 4.2 copy.78
  31.1 11.9 %broadcast_select_fusion.1 = f32[8,8,193,16]{3,1,2,0:T(8,128)} fusion(pred[8,193]{0,1:T(8,128)(4,1)S(1)} %copy-done.4, bf16[16,16,5,5]{1,0,3,2:T(8,128)(2,1)S(1)} %copy-done, bf16[16,12,1,7,4]{0,3,4,1,2:T(8,128)(2,1)S(1)} %slice.206, bf16[16,12,1,8,193]{0,3,4,1,2:T(8,128)(2,1)} %copy.78), kind=kOutput, calls=%fused_computation.126 | convolution fusion | flops 160118784 | bytes 1408520 | tf_op jit(solution)/shard_map/conv_general_dilated | solution.py:95
  43.0 5.0 %copy.79 = f32[8,8,193,16]{2,1,3,0:T(8,128)S(1)} copy(f32[8,8,193,16]{3,1,2,0:T(8,128)} %broadcast_select_fusion.1) | data formatting | bytes 1581056 | tf_op jit(solution)/shard_map/conv_general_dilated | solution.py:95
  48.5 1.8 fusion.53
  50.3 1.9 collective-permute-start.2
  52.2 2.6 collective-permute-start.3
  54.9 3.3 collective-permute-done.3
  60.3 4.2 copy.81
  65.4 11.9 %broadcast_select_fusion = f32[8,8,193,16]{3,1,2,0:T(8,128)} fusion(pred[8,193]{0,1:T(8,128)(4,1)S(1)} %copy-done.4, bf16[16,16,5,5]{1,0,3,2:T(8,128)(2,1)S(1)} %copy-done.3, bf16[16,12,1,7,4]{0,3,4,1,2:T(8,128)(2,1)S(1)} %slice.212, bf16[16,12,1,8,193]{0,3,4,1,2:T(8,128)(2,1)} %copy.81), kind=kOutput, calls=%fused_computation.125 | convolution fusion | flops 160118784 | bytes 1408520 | tf_op jit(solution)/shard_map/conv_general_dilated | solution.py:95
  77.3 5.1 %copy.82 = f32[8,8,193,16]{2,1,3,0:T(8,128)S(1)} copy(f32[8,8,193,16]{3,1,2,0:T(8,128)} %broadcast_select_fusion) | data formatting | bytes 1581056 | tf_op jit(solution)/shard_map/conv_general_dilated | solution.py:95
  83.0 1.6 fusion.50
  84.6 1.9 collective-permute-start.4
  87.7 1.9 collective-permute-start.5
  89.8 2.6 collective-permute-done.5
  92.4 7.5 %collective-permute-start.6 = (bf16[16,4,2,128]{3,0,2,1:T(8,128)(2,1)S(1)}, bf16[16,4,2,128]{3,0,2,1:T(8,128)(2,1)S(1)}, u32[]{:S(2)}, u32[]{:S(2)}) collective-permute-start(bf16[16,4,2,128]{3,0,2,1:T(8,128)(2,1)S(1)} %collective-permute-done.5), channel_id=1, source_target_pairs={{0,64},{16,80},{32,96},{48,112},{64,0},{80,16},{96,32},{112,48},{1... | collective-permute-start | bytes 98312 | tf_op jit(solution)/shard_map/ppermute | solution.py:28
  99.9 209.0 %while.19 = (s32[]{:T(128)}, f32[128,4]{0,1:T(4,128)S(1)}, f32[128,4]{0,1:T(4,128)S(1)}, f32[16,16,128,4]{2,3,1,0:T(4,128)S(1)}, s32[16,16]{1,0:T(8,128)S(1)}, /...) while((s32[]{:T(128)}, f32[128,4]{0,1:T(4,128)S(1)}, ...), condition=%wide.region_1.2_spmd.clone.clone, body=%wide.region_0.1_spmd.clone.clone.sunk | while | flops 93906 | bytes 283852 | solution.py:70
  308.9 4.0 collective-permute-start.7
  314.2 5.2 %collective-permute-start.8 = (bf16[16,4,2,128]{3,0,2,1:T(8,128)(2,1)S(1)}, bf16[16,4,2,128]{3,0,2,1:T(8,128)(2,1)S(1)}, u32[]{:S(2)}, u32[]{:S(2)}) collective-permute-start(bf16[16,4,2,128]{3,0,2,1:T(8,128)(2,1)S(1)} %collective-permute-done.7), channel_id=1, source_target_pairs={{0,256},{16,272},{32,288},{48,304},{64,320},{80,336},{96,352},{112... | collective-permute-start | bytes 98312 | tf_op jit(solution)/shard_map/ppermute | solution.py:28
  321.1 3.4 fusion.72
  324.5 152.1 %reduce-scatter.2.cloned.1.call-done = f32[4,2,16,2,128]{4,2,3,1,0:T(8,128)} async-done(((f32[128,2,16,2,128]{4,2,3,1,0:T(8,128)}), f32[4,2,16,2,128]{4,2,3,1,0:T(8,128)}) %reduce-scatter.2.cloned.1.call-update) | async-done | bytes 131088 | tf_op jit(solution)/shard_map/reduce_scatter | solution.py:149
  476.6 1.6 copy.91
  (885 shorter events, 55.8 us)
Async XLA Ops:
  6.5 24.5 %copy-start = (bf16[16,16,5,5]{1,0,3,2:T(8,128)(2,1)S(1)}, bf16[16,16,5,5]{1,0,3,2:T(8,128)(2,1)}, u32[]{:S(2)}) copy-start(bf16[16,16,5,5]{1,0,3,2:T(8,128)(2,1)} %param.7) | copy-start | bytes 38404
  6.5 470.1 %reduce-scatter.2.cloned.1.call-start = ((), (), s32[]{:S(2)}) async-start(), calls=%async_computation.1 | async-start | bytes 4325376 | tf_op jit(solution)/shard_map/reduce_scatter | solution.py:149
  7.8 14.3 %collective-permute-start = (bf16[16,2,1536]{2,1,0:T(2,128)(2,1)S(1)}, bf16[16,2,1536]{2,1,0:T(2,128)(2,1)S(1)}, u32[]{:S(2)}, u32[]{:S(2)}) collective-permute-start(bf16[16,2,1536]{2,1,0:T(2,128)(2,1)S(1)} %get-tuple-element.665), channel_id=1, source_target_pairs={{0,16},{16,32},{32,48},{48,64},{64,80},{80,96},{96,112},{112,128},... | collective-permute-start | bytes 294920 | tf_op jit(solution)/shard_map/ppermute | solution.py:19
  12.4 9.8 %collective-permute-start.1 = (bf16[16,2,1536]{2,1,0:T(2,128)(2,1)S(1)}, bf16[16,2,1536]{2,1,0:T(2,128)(2,1)S(1)}, u32[]{:S(2)}, u32[]{:S(2)}) collective-permute-start(bf16[16,2,1536]{2,1,0:T(2,128)(2,1)S(1)} %get-tuple-element.666), channel_id=1, source_target_pairs={{16,0},{32,16},{48,32},{64,48},{80,64},{96,80},{112,96},{128,112},... | collective-permute-start | bytes 294920 | tf_op jit(solution)/shard_map/ppermute | solution.py:20
  24.5 6.6 %copy-start.4 = (pred[8,193]{0,1:T(8,128)(4,1)S(1)}, pred[8,193]{0,1:T(8,128)(4,1)}, u32[]{:S(2)}) copy-start(pred[8,193]{0,1:T(8,128)(4,1)} %constant.274) | copy-start | bytes 4636
  43.0 5.5 %copy-start.2 = (f32[16]{0:T(128)S(1)}, f32[16]{0:T(128)}, u32[]{:S(2)}) copy-start(f32[16]{0:T(128)} %param.8) | copy-start | bytes 196
  50.3 4.6 collective-permute-start.2
  52.2 5.9 %collective-permute-start.3 = (bf16[16,2,1536]{2,0,1:T(8,128)(2,1)S(1)}, bf16[16,2,1536]{2,0,1:T(8,128)(2,1)S(1)}, u32[]{:S(2)}, u32[]{:S(2)}) collective-permute-start(bf16[16,2,1536]{2,0,1:T(8,128)(2,1)S(1)} %get-tuple-element.664), channel_id=1, source_target_pairs={{16,0},{32,16},{48,32},{64,48},{80,64},{96,80},{112,96},{128,112},... | collective-permute-start | bytes 294920 | tf_op jit(solution)/shard_map/ppermute | solution.py:20
  58.3 7.1 %copy-start.3 = (bf16[16,16,5,5]{1,0,3,2:T(8,128)(2,1)S(1)}, bf16[16,16,5,5]{1,0,3,2:T(8,128)(2,1)}, u32[]{:S(2)}) copy-start(bf16[16,16,5,5]{1,0,3,2:T(8,128)(2,1)} %param.9) | copy-start | bytes 38404
  77.3 5.5 %copy-start.1 = (bf16[16,8,1536]{2,1,0:T(8,128)(2,1)S(1)}, bf16[16,8,1536]{2,1,0:T(8,128)(2,1)}, u32[]{:S(2)}) copy-start(bf16[16,8,1536]{2,1,0:T(8,128)(2,1)} %param.6) | copy-start | bytes 1179652
  84.6 3.1 collective-permute-start.4
  87.7 4.6 collective-permute-start.5
  92.4 216.5 %collective-permute-start.6 = (bf16[16,4,2,128]{3,0,2,1:T(8,128)(2,1)S(1)}, bf16[16,4,2,128]{3,0,2,1:T(8,128)(2,1)S(1)}, u32[]{:S(2)}, u32[]{:S(2)}) collective-permute-start(bf16[16,4,2,128]{3,0,2,1:T(8,128)(2,1)S(1)} %collective-permute-done.5), channel_id=1, source_target_pairs={{0,64},{16,80},{32,96},{48,112},{64,0},{80,16},{96,32},{112,48},{1... | collective-permute-start | bytes 98312 | tf_op jit(solution)/shard_map/ppermute | solution.py:28
  308.9 5.3 %collective-permute-start.7 = (bf16[16,4,2,128]{3,0,2,1:T(8,128)(2,1)S(1)}, bf16[16,4,2,128]{3,0,2,1:T(8,128)(2,1)S(1)}, u32[]{:S(2)}, u32[]{:S(2)}) collective-permute-start(bf16[16,4,2,128]{3,0,2,1:T(8,128)(2,1)S(1)} %collective-permute-done.6), channel_id=1, source_target_pairs={{0,128},{16,144},{32,160},{48,176},{64,192},{80,208},{96,224},{112... | collective-permute-start | bytes 98312 | tf_op jit(solution)/shard_map/ppermute | solution.py:28
  314.2 6.5 %collective-permute-start.8 = (bf16[16,4,2,128]{3,0,2,1:T(8,128)(2,1)S(1)}, bf16[16,4,2,128]{3,0,2,1:T(8,128)(2,1)S(1)}, u32[]{:S(2)}, u32[]{:S(2)}) collective-permute-start(bf16[16,4,2,128]{3,0,2,1:T(8,128)(2,1)S(1)} %collective-permute-done.7), channel_id=1, source_target_pairs={{0,256},{16,272},{32,288},{48,304},{64,320},{80,336},{96,352},{112... | collective-permute-start | bytes 98312 | tf_op jit(solution)/shard_map/ppermute | solution.py:28
Sparse Core Ops, SparseCore 0:
  324.6 151.9 reduce-scatter.1
where the time goes:
time: 492 us; the launch traced here: 485 us
  loops' own time  168 us (34%)
  waiting for transfers between devices  161 us (33%)
  local copies, waits for them, and re-layouts  41 us (8%)
  other arithmetic  37.6 us (8%)
  starting transfers between devices  35.1 us (7%)
  matrix products  28.7 us (6%)
  between operations  13.8 us (3%)
    another operation x1, loops' own time, legendre(): lax.scan(advance, (empty_rows, empty_rows), jnp.arange(degrees, dtype=jnp...  168 us
    reduce_scatter x1, waiting for transfers between devices, per_device(): lax.psum_scatter(project(even_sum, odd_sum, spherical_all, numbers), 'lat...  152 us
    conv_general_dilated x10, local copies, waits for them, and re-layouts, convolve(): lax.conv_general_dilated(widened[None], kernel, (1, 1), 'VALID', feature_...  23.8 us
    conv_general_dilated x2, matrix products, convolve(): lax.conv_general_dilated(widened[None], kernel, (1, 1), 'VALID', feature_...  23.8 us
    while x240, other arithmetic  20.5 us
    ppermute x5, starting transfers between devices, partner(): return lax.ppermute(value, axis, pairs)  20.5 us
    slice x16, local copies, waits for them, and re-layouts, legendre(): lax.scan(advance, (empty_rows, empty_rows), jnp.arange(degrees, dtype=jnp...  11.5 us
  transfers between devices with their start and end apart: 10, of which 6 were waited for; matrix products, arithmetic and copies ran while one was open for 10% of the time, Pallas kernels for 0%

commit v1 on v0

v1 whole, which is shorter than its diff:
```python
import functools
import math

import jax
import jax.numpy as jnp
import numpy as np
from jax import lax
from jax.experimental import pallas as pl
from jax.experimental.pallas import tpu as pltpu
from jax.sharding import PartitionSpec as P

ORDERS = 128
DEGREES = 256
LAT = 256
LON = 1536
BANDS = 32
ROWS = 8
CH = 16
OWN = ORDERS // BANDS
BF16 = jnp.bfloat16
F32 = jnp.float32


def fourier_rows():
    orders = np.arange(1, ORDERS + 1)
    places = np.arange(LON)
    phases = (orders[:, None] * places[None, :] % LON) * (2.0 * math.pi / LON)
    real = np.cos(phases) / math.sqrt(LON)
    imag = -np.sin(phases) / math.sqrt(LON)
    both = np.stack([real.reshape(BANDS, OWN, LON), imag.reshape(BANDS, OWN, LON)], axis=1)
    return both.reshape(2 * ORDERS, LON).astype(BF16)


def phase_rows():
    orders = np.arange(1, ORDERS + 1).reshape(BANDS, OWN)
    out = []
    for step in (1, 2):
        angle = 2.0 * math.pi * step * orders / LON
        cosine = np.stack([np.cos(angle), np.cos(angle)], axis=1).reshape(2 * ORDERS)
        sine = np.stack([-np.sin(angle), np.sin(angle)], axis=1).reshape(2 * ORDERS)
        out += [cosine, sine]
    table = np.stack(out)[:, :, None]
    return np.broadcast_to(table, (4, 2 * ORDERS, 128)).astype(np.float32).copy()


def projection_table():
    half = LAT // 2
    single = np.float32
    theta = (math.pi * (np.arange(half) + 0.5) / LAT).astype(single)
    cosine, sine = np.cos(theta)[None, :], np.sin(theta)[None, :]
    order = np.arange(1, ORDERS + 1, dtype=single)[:, None]
    gamma = np.vectorize(math.lgamma, otypes=[single])
    log_diag = (
        single(0.5)
        * (
            np.log((2 * order + 1) / 2)
            + gamma(2 * order + 1)
            - order * single(math.log(4.0))
            - 2 * gamma(order + 1)
        )
        + order * np.log(sine)
    )

    def normal(value):
        return np.where(np.abs(value) < np.finfo(single).tiny, single(0.0), value)

    diagonal = normal(np.exp(log_diag))
    latest = np.zeros_like(diagonal)
    before = np.zeros_like(diagonal)
    stacked = np.zeros((DEGREES, ORDERS, half), single)
    for degree in range(DEGREES):
        real = single(degree)
        spread = np.maximum(real * real - order * order, single(1.0))
        raising = np.sqrt(np.maximum(4 * real * real - 1, single(1.0)) / spread)
        previous = real - 1
        lowering = np.sqrt(
            np.maximum(previous * previous - order * order, single(0.0))
            / np.maximum(4 * previous * previous - 1, single(1.0))
        )
        raised = normal(
            raising * normal(normal(cosine * latest) - normal(lowering * before))
        )
        result = np.where(order == real, diagonal, np.where(order < real, raised, single(0.0)))
        stacked[degree] = result
        latest, before = result, latest
    weighted = stacked * (single(math.pi) * sine / single(math.sqrt(LAT)))[None]
    weighted = weighted.astype(BF16).astype(single)
    degrees = np.arange(DEGREES)[:, None, None]
    numbers = np.arange(1, ORDERS + 1)[None, :, None]
    sign = np.where((degrees + numbers) % 2 == 0, 1.0, -1.0).astype(np.float32)
    whole = np.concatenate([weighted, (weighted * sign)[:, :, ::-1]], axis=2)
    whole = whole.reshape(DEGREES // 2, 2, ORDERS, LAT).transpose(2, 3, 1, 0)
    return whole.reshape(BANDS, OWN, LAT, DEGREES).astype(BF16)


EDGE = (0, 1, 6, 7)
SLOTS = (0, 1, 2, 3, 4, 5, 6, 7, 8, 9, -2, -1)


def spread_first():
    own = np.zeros((128, ROWS, CH, ROWS), np.float32)
    halo = np.zeros((128, 4, 2, CH, 2), np.float32)
    for dy in range(5):
        for i in range(CH):
            for y in range(ROWS):
                row = y + dy - 2
                if 0 <= row < ROWS:
                    own[dy * CH + i, y, i, row] = 1.0
                elif row < 0:
                    halo[dy * CH + i, EDGE.index(y), 0, i, row + 2] = 1.0
                else:
                    halo[dy * CH + i, EDGE.index(y), 1, i, row - ROWS] = 1.0
    return np.concatenate([own.reshape(128, -1), halo.reshape(128, -1)], axis=1).astype(BF16)


def spread_second():
    out = np.zeros((128, len(SLOTS), ROWS, CH), np.float32)
    for dy in range(5):
        for i in range(CH):
            for at, slot in enumerate(SLOTS):
                row = slot + dy - 2
                if 0 <= row < ROWS:
                    out[dy * CH + i, at, row, i] = 1.0
    return out.reshape(128, -1).astype(BF16)


def edge_rows():
    out = np.zeros((2, CH, 2, CH, ROWS), np.float32)
    for c in range(CH):
        for t in range(2):
            out[0, c, t, c, t] = 1.0
            out[1, c, t, c, ROWS - 2 + t] = 1.0
    return out.reshape(64, 128).astype(BF16)


def placed_rows():
    out = np.zeros((16, CH, CH, ROWS), np.float32)
    for c in range(CH):
        for y in range(ROWS):
            out[y, c, c, y] = 1.0
    return out.reshape(256, 128).astype(BF16)


def nt(a, b):
    return lax.dot_general(a, b, (((1,), (1,)), ((), ())), preferred_element_type=F32)


def gelu(x):
    return 0.5 * x * (1.0 + lax.erf(x * math.sqrt(0.5)))


def swap_blocks(x):
    sub = lax.broadcasted_iota(jnp.int32, x.shape, 1)
    block = lax.broadcasted_iota(jnp.int32, x.shape, 2) // CH
    for bit in (1, 2, 4):
        high_sub = (sub & bit) != 0
        high_block = (block & bit) != 0
        lane = CH * bit
        down = pltpu.roll(pltpu.roll(x, 8 - bit, 1), lane, 2)
        up = pltpu.roll(pltpu.roll(x, bit, 1), 128 - lane, 2)
        x = jnp.where(high_sub == high_block, x, jnp.where(high_sub, up, down))
    return x


def base_of(weight):
    pieces = [weight[dy].reshape(5 * CH, CH).astype(F32) for dy in range(5)]
    pieces.append(jnp.zeros((5 * CH, 128 - 5 * CH), F32))
    return jnp.concatenate(pieces, axis=1).astype(BF16)


def kernel(
    atm, w1, bias, w2, edge, spread1, spread2, placed, fourier, phase, table, out,
    shifted, halo, w1_v, bias_v, w2_v, edge_v, spread1_v, spread2_v, fourier_v, phase_v, table_v,
    t1, t1h, t2, hsend, acc, hidden, mixed, packed, received, result,
    load_sem, halo_send, halo_recv, a2a_send, a2a_recv, out_sem,
):
    me = lax.axis_index("lat")
    barrier = pltpu.get_barrier_semaphore()

    loads = [
        (atm, shifted.at[pl.ds(256, 128), :]),
        (edge, edge_v),
        (w1, w1_v),
        (spread1, spread1_v),
        (bias, bias_v),
        (w2, w2_v),
        (spread2, spread2_v),
        (fourier, fourier_v),
        (placed, t2.at[:, pl.ds(640, 128)]),
        (phase, phase_v),
        (table.at[me], table_v),
    ]
    copies = [
        pltpu.make_async_copy(source, target, load_sem.at[n])
        for n, (source, target) in enumerate(loads)
    ]
    for copy in copies:
        copy.start()

    def greet(j, carry):
        pl.semaphore_signal(
            barrier, inc=1, device_id={"lat": lax.rem(me + j, BANDS)},
            device_id_type=pl.DeviceIdType.MESH,
        )
        return carry

    lax.fori_loop(1, BANDS, greet, 0)

    copies[0].wait()
    copies[1].wait()
    hsend[...] = jnp.dot(
        edge_v[...], shifted[256:384, :], preferred_element_type=F32
    ).astype(BF16)

    pl.semaphore_wait(barrier, BANDS - 1)

    up = lax.max(me - 1, 0)
    down = lax.min(me + 1, BANDS - 1)
    to_up = pltpu.make_async_remote_copy(
        src_ref=hsend.at[pl.ds(0, 32), :], dst_ref=halo.at[pl.ds(160, 32), :],
        send_sem=halo_send.at[0], recv_sem=halo_recv.at[0],
        device_id={"lat": up}, device_id_type=pl.DeviceIdType.MESH,
    )
    to_down = pltpu.make_async_remote_copy(
        src_ref=hsend.at[pl.ds(32, 32), :], dst_ref=halo.at[pl.ds(128, 32), :],
        send_sem=halo_send.at[1], recv_sem=halo_recv.at[1],
        device_id={"lat": down}, device_id_type=pl.DeviceIdType.MESH,
    )

    @pl.when(me > 0)
    def _():
        to_up.start()

    @pl.when(me < BANDS - 1)
    def _():
        to_down.start()

    copies[2].wait()
    copies[3].wait()
    res1 = jnp.dot(base_of(w1_v), spread1_v[...], preferred_element_type=F32).astype(BF16)
    for dx in range(5):
        for y in range(ROWS):
            t1[16 * y : 16 * y + 16, 128 * dx : 128 * dx + 128] = res1[
                16 * dx : 16 * dx + 16, 128 * y : 128 * y + 128
            ]
        for e in range(4):
            t1h[16 * e : 16 * e + 16, 64 * dx : 64 * dx + 64] = res1[
                16 * dx : 16 * dx + 16, 1024 + 64 * e : 1088 + 64 * e
            ]

    own = shifted[256:384, :].astype(F32)
    for dx in (0, 1, 3, 4):
        shifted[128 * dx : 128 * dx + 128, :] = pltpu.roll(own, (2 - dx) % LON, 1).astype(BF16)
    copies[4].wait()
    eye = lax.broadcasted_iota(jnp.int32, (CH, CH), 0) == lax.broadcasted_iota(
        jnp.int32, (CH, CH), 1
    )
    column = jnp.sum(
        jnp.where(eye, jnp.broadcast_to(bias_v[...], (CH, CH)), 0.0), axis=1, keepdims=True
    )
    offsets = jnp.concatenate([column] * ROWS, axis=0)
    acc[...] = jnp.dot(t1[...], shifted[...], preferred_element_type=F32) + offsets
    hidden[32:96, :] = gelu(acc[32:96, :]).astype(BF16)

    copies[5].wait()
    copies[6].wait()
    res2 = jnp.dot(base_of(w2_v), spread2_v[...], preferred_element_type=F32).astype(BF16)
    for at, slot in enumerate(SLOTS):
        row = 16 * (slot % 16)
        for dx in range(5):
            t2[row : row + 16, 128 * dx : 128 * dx + 128] = res2[
                16 * dx : 16 * dx + 16, 128 * at : 128 * at + 128
            ]
    t2[160:224, 0:640] = jnp.zeros((64, 640), BF16)
    copies[7].wait()
    mixed[:, 640:768] = nt(fourier_v[...], shifted[256:384, :]).astype(BF16)

    @pl.when(me > 0)
    def _():
        to_up.wait_send()
        to_down.wait_recv()

    @pl.when(me < BANDS - 1)
    def _():
        to_down.wait_send()
        to_up.wait_recv()

    @pl.when(me == 0)
    def _():
        halo[128:160, :] = jnp.zeros((32, LON), BF16)

    @pl.when(me == BANDS - 1)
    def _():
        halo[160:192, :] = jnp.zeros((32, LON), BF16)

    rim = halo[128:192, :].astype(F32)
    for dx in (0, 1, 3, 4):
        halo[64 * dx : 64 * dx + 64, :] = pltpu.roll(rim, (2 - dx) % LON, 1).astype(BF16)
    more = jnp.dot(t1h[...], halo[...], preferred_element_type=F32)
    hidden[0:32, :] = gelu(acc[0:32, :] + more[0:32]).astype(BF16)
    hidden[96:128, :] = gelu(acc[96:128, :] + more[32:64]).astype(BF16)

    spectra = nt(fourier_v[...], hidden[...])
    swapped = pltpu.roll(spectra.reshape(BANDS, 8, 128), 4, 1).reshape(256, 128)
    copies[9].wait()
    mixed[:, 256:384] = spectra.astype(BF16)
    for step, low, high in ((1, 1, 3), (2, 0, 4)):
        straight = phase_v[2 * step - 2] * spectra
        crossed = phase_v[2 * step - 1] * swapped
        mixed[:, 128 * high : 128 * high + 128] = (straight + crossed).astype(BF16)
        mixed[:, 128 * low : 128 * low + 128] = (straight - crossed).astype(BF16)

    copies[8].wait()
    sums = nt(mixed[...], t2[...]).reshape(BANDS, 8, 256)
    near = swap_blocks(sums[:, :, 0:128])
    far = swap_blocks(sums[:, :, 128:256])
    packed[...] = jnp.concatenate([near, far], axis=1).astype(BF16)

    def send(j, carry):
        p = lax.rem(me + j, BANDS)
        pltpu.make_async_remote_copy(
            src_ref=packed.at[p], dst_ref=received.at[me],
            send_sem=a2a_send, recv_sem=a2a_recv,
            device_id={"lat": p}, device_id_type=pl.DeviceIdType.MESH,
        ).start()
        return carry

    lax.fori_loop(1, BANDS, send, 0)
    received[me] = packed[me]
    copies[10].wait()
    some = pltpu.make_async_remote_copy(
        src_ref=packed.at[pl.ds(0, BANDS - 1)], dst_ref=received.at[pl.ds(0, BANDS - 1)],
        send_sem=a2a_send, recv_sem=a2a_recv,
        device_id={"lat": lax.rem(me + 1, BANDS)}, device_id_type=pl.DeviceIdType.MESH,
    )
    some.wait_recv()

    parts = received[...].astype(F32)
    near = parts[:, 0:8, :]
    far = parts[:, 8:16, :]
    none = jnp.zeros((1, 8, 128), F32)
    above = jnp.concatenate([none, far[:-1]], axis=0)
    below = jnp.concatenate([far[1:], none], axis=0)
    first = lax.broadcasted_iota(jnp.int32, near.shape, 1) < 4
    rows = (near + jnp.where(first, above, below)).reshape(LAT, 128)
    lines = rows.T.astype(BF16)
    for m in range(OWN):
        left = jnp.concatenate([lines[16 * m : 16 * m + 16], lines[64 + 16 * m : 80 + 16 * m]], axis=0)
        done = jnp.dot(left, table_v[m], preferred_element_type=F32)
        for q in range(2):
            for a in range(2):
                result[m, q, pl.ds(a, CH, stride=2), :] = done[
                    16 * a : 16 * a + 16, 128 * q : 128 * q + 128
                ]
    finish = pltpu.make_async_copy(result, out, out_sem)
    finish.start()
    finish.wait()
    some.wait_send()


@functools.cache
def constants():
    return (
        edge_rows(), spread_first(), spread_second(), placed_rows(), fourier_rows(),
        phase_rows(), projection_table(),
    )


def per_device(atmosphere, first_weight, first_bias, second_weight):
    edge, spread1, spread2, placed, fourier, phase, table = constants()
    operands = (
        atmosphere.reshape(CH * ROWS, LON),
        first_weight.transpose(2, 3, 0, 1),
        first_bias.reshape(1, CH),
        second_weight.transpose(2, 3, 0, 1),
        edge, spread1, spread2, placed, fourier, phase, table,
    )
    scratch = [
        pltpu.VMEM((640, LON), BF16),
        pltpu.VMEM((320, LON), BF16),
        pltpu.VMEM((5, 5, CH, CH), BF16),
        pltpu.VMEM((1, CH), F32),
        pltpu.VMEM((5, 5, CH, CH), BF16),
        pltpu.VMEM(edge.shape, BF16),
        pltpu.VMEM(spread1.shape, BF16),
        pltpu.VMEM(spread2.shape, BF16),
        pltpu.VMEM(fourier.shape, BF16),
        pltpu.VMEM(phase.shape, F32),
        pltpu.VMEM(table.shape[1:], BF16),
        pltpu.VMEM((128, 640), BF16),
        pltpu.VMEM((64, 320), BF16),
        pltpu.VMEM((256, 768), BF16),
        pltpu.VMEM((64, LON), BF16),
        pltpu.VMEM((128, LON), F32),
        pltpu.VMEM((128, LON), BF16),
        pltpu.VMEM((256, 768), BF16),
        pltpu.VMEM((BANDS, 16, 128), BF16),
        pltpu.VMEM((BANDS, 16, 128), BF16),
        pltpu.VMEM((OWN, 2, 2 * CH, 128), F32),
        pltpu.SemaphoreType.DMA((11,)),
        pltpu.SemaphoreType.DMA((2,)),
        pltpu.SemaphoreType.DMA((2,)),
        pltpu.SemaphoreType.DMA,
        pltpu.SemaphoreType.DMA,
        pltpu.SemaphoreType.DMA,
    ]
    spectrum = pl.pallas_call(
        kernel,
        out_shape=jax.ShapeDtypeStruct((OWN, 2, 2 * CH, 128), F32),
        in_specs=[pl.BlockSpec(memory_space=pl.ANY)] * len(operands),
        out_specs=pl.BlockSpec(memory_space=pl.ANY),
        scratch_shapes=scratch,
        compiler_params=pltpu.CompilerParams(
            collective_id=0, has_side_effects=True, vmem_limit_bytes=56 * 1024 * 1024
        ),
        name="encoder",
    )(*operands)
    return spectrum.reshape(OWN, 2, CH, 2, 128)


def solution(mesh):
    placed = (
        P("chan", "lat", None),
        P("chan", None, None, None),
        P("chan"),
        P("chan", None, None, None),
    )
    return jax.shard_map(
        per_device,
        mesh=mesh,
        in_specs=placed,
        out_specs=P("lat", None, "chan", None, None),
        check_vma=False,
    )
```

time: 492 us -> 22.7 us (0.05); the launches traced: 485 us -> 22.6 us
  loops' own time: 168 us -> 0 us
  waiting for transfers between devices: 161 us -> 0 us
  local copies, waits for them, and re-layouts: 41 us -> 1.57 us
  other arithmetic: 37.6 us -> 0 us
  starting transfers between devices: 35.1 us -> 0 us
  matrix products: 28.7 us -> 0 us
  Pallas kernels: 0 us -> 21 us
  between operations: 13.8 us -> 0.01 us
    another operation x1 -> x0, loops' own time: 168 us -> none  [legendre(): lax.scan(advance, (empty_rows, empty_rows), jnp.arange(degrees, dtype=jnp...]
    reduce_scatter x1 -> x0, waiting for transfers between devices: 152 us -> none  [per_device(): lax.psum_scatter(project(even_sum, odd_sum, spherical_all, numbers), 'lat...]
    ppermute x9 -> x0, starting transfers between devices: 35.1 us -> none  [the longest x5 20.5 us: partner(): return lax.ppermute(value, axis, pairs)]
    conv_general_dilated x10 -> x0, local copies, waits for them, and re-layouts: 23.8 us -> none  [convolve(): lax.conv_general_dilated(widened[None], kernel, (1, 1), 'VALID', feature_...]
    conv_general_dilated x2 -> x0, matrix products: 23.8 us -> none  [convolve(): lax.conv_general_dilated(widened[None], kernel, (1, 1), 'VALID', feature_...]
    pallas_call x0 -> x1, Pallas kernels: none -> 21 us  [per_device(): pl.pallas_call(kernel, out_shape=jax.ShapeDtypeStruct((OWN, 2, 2 * CH, 12...]
    while x240 -> x0, other arithmetic: 20.5 us -> none
    slice x21 -> x0, local copies, waits for them, and re-layouts: 13 us -> none  [the longest x16 11.5 us: legendre(): lax.scan(advance, (empty_rows, empty_rows), jnp.arange(degrees, dtype=jnp...]
  transfers between devices with their start and end apart: 10 -> 0, of which waited for: 6 -> 0; matrix products, arithmetic and copies ran while one was open for 10% -> 0% of each run, Pallas kernels for 0% -> 0%
where the time goes in v1:
time: 22.7 us; the launch traced here: 22.6 us
  Pallas kernels  21 us (93%)
  local copies, waits for them, and re-layouts  1.57 us (7%)
    pallas_call x1, Pallas kernels, per_device(): pl.pallas_call(kernel, out_shape=jax.ShapeDtypeStruct((OWN, 2, 2 * CH, 12...  21 us
    unnamed x1, local copies, waits for them, and re-layouts  1.57 us

profile of v1, /device:TPU:1, one launch (start us, length us, event | category | flops | bytes accessed | tf_op | source)
XLA Modules:
  0.0 22.6 jit_solution(18242060105579505279)
XLA Ops:
  0.0 21.0 %encoder.1 = f32[4,2,32,128]{3,2,1,0:T(8,128)} custom-call(bf16[128,1536]{1,0:T(8,128)(2,1)} %bitcast.6, bf16[5,5,16,16]{3,2,1,0:T(8,128)(2,1)} %bitcast.7, f32[1,16]{1,0:T(1,128)} %bitcast.9, bf16[5,5,16,16]{3,2,1,0:T(8,128)(2,1)} %bitcast.8, bf16[64,128]{1,0:T(8,128)(2,1)} %constant.14.clone.edge, bf16[128,1280]{1,0:T(8,128)(2,1)} %constant.15.clone.spread1, ...), custom_call_target="tpu_custom_call" | custom-call | tf_op jit(solution)/shard_map/encoder/pallas_call | solution.py:407
  21.0 1.6 %copy.13 = f32[4,2,16,2,128]{4,3,2,1,0:T(2,128)} copy(f32[4,2,16,2,128]{4,3,2,1,0:T(2,128)} %bitcast.5) | data formatting | bytes 262144

commit v2 on v1

--- a/solution.py
+++ b/solution.py
@@ -168,11 +168,29 @@
     return jnp.concatenate(pieces, axis=1).astype(BF16)
 
 
+def peers(me):
+    z, x, core = me // 8, (me // 2) % 4, me % 2
+    depths = [(3, 3 - z), (2, (z + 2) % 4), (1, (z // 2) * 2 + 1 - z % 2), (0, z)]
+    widths = [(2, (x + 2) % 4), (1, (x + 1) % 4), (1, (x + 3) % 4), (0, x)]
+    pairs = sorted(
+        ((far + wide, far, n, depth, width)
+         for far, depth in depths
+         for n, (wide, width) in enumerate(widths)),
+        key=lambda pair: (-pair[0], -pair[1], pair[2]),
+    )
+    found = []
+    for total, _, _, depth, width in pairs:
+        for twin in (1 - core, core):
+            if total > 0 or twin is not core:
+                found.append((depth * 4 + width) * 2 + twin)
+    return found
+
+
 def kernel(
-    atm, w1, bias, w2, edge, spread1, spread2, placed, fourier, phase, table, out,
+    atm, w1, bias, w2, edge, spread1, spread2, placed, fourier, phase, table, result,
     shifted, halo, w1_v, bias_v, w2_v, edge_v, spread1_v, spread2_v, fourier_v, phase_v, table_v,
-    t1, t1h, t2, hsend, acc, hidden, mixed, packed, received, result,
-    load_sem, halo_send, halo_recv, a2a_send, a2a_recv, out_sem,
+    t1, t1h, t2, hsend, acc, hidden, mixed, packed, received,
+    load_sem, halo_send, halo_recv, a2a_send, a2a_recv,
 ):
     me = lax.axis_index("lat")
     barrier = pltpu.get_barrier_semaphore()
@@ -197,6 +215,12 @@
     for copy in copies:
         copy.start()
 
+    others = peers(me)
+    for other in [lax.rem(me + 1, BANDS), lax.rem(me + BANDS - 1, BANDS)]:
+        pl.semaphore_signal(
+            barrier, inc=1, device_id={"lat": other}, device_id_type=pl.DeviceIdType.MESH
+        )
+
     def greet(j, carry):
         pl.semaphore_signal(
             barrier, inc=1, device_id={"lat": lax.rem(me + j, BANDS)},
@@ -204,7 +228,7 @@
         )
         return carry
 
-    lax.fori_loop(1, BANDS, greet, 0)
+    lax.fori_loop(2, BANDS - 1, greet, 0)
 
     copies[0].wait()
     copies[1].wait()
@@ -316,16 +340,12 @@
     far = swap_blocks(sums[:, :, 128:256])
     packed[...] = jnp.concatenate([near, far], axis=1).astype(BF16)
 
-    def send(j, carry):
-        p = lax.rem(me + j, BANDS)
+    for p in others:
         pltpu.make_async_remote_copy(
             src_ref=packed.at[p], dst_ref=received.at[me],
             send_sem=a2a_send, recv_sem=a2a_recv,
             device_id={"lat": p}, device_id_type=pl.DeviceIdType.MESH,
         ).start()
-        return carry
-
-    lax.fori_loop(1, BANDS, send, 0)
     received[me] = packed[me]
     copies[10].wait()
     some = pltpu.make_async_remote_copy(
@@ -352,10 +372,13 @@
                 result[m, q, pl.ds(a, CH, stride=2), :] = done[
                     16 * a : 16 * a + 16, 128 * q : 128 * q + 128
                 ]
-    finish = pltpu.make_async_copy(result, out, out_sem)
-    finish.start()
-    finish.wait()
     some.wait_send()
+
+
+def store(source, target, semaphore):
+    copy = pltpu.make_async_copy(source, target, semaphore)
+    copy.start()
+    copy.wait()
 
 
 @functools.cache
@@ -396,25 +419,31 @@
         pltpu.VMEM((256, 768), BF16),
         pltpu.VMEM((BANDS, 16, 128), BF16),
         pltpu.VMEM((BANDS, 16, 128), BF16),
-        pltpu.VMEM((OWN, 2, 2 * CH, 128), F32),
         pltpu.SemaphoreType.DMA((11,)),
         pltpu.SemaphoreType.DMA((2,)),
         pltpu.SemaphoreType.DMA((2,)),
-        pltpu.SemaphoreType.DMA,
         pltpu.SemaphoreType.DMA,
         pltpu.SemaphoreType.DMA,
     ]
     spectrum = pl.pallas_call(
         kernel,
         out_shape=jax.ShapeDtypeStruct((OWN, 2, 2 * CH, 128), F32),
-        in_specs=[pl.BlockSpec(memory_space=pl.ANY)] * len(operands),
-        out_specs=pl.BlockSpec(memory_space=pl.ANY),
+        in_specs=[pl.BlockSpec(memory_space=pltpu.HBM)] * len(operands),
+        out_specs=pl.BlockSpec(memory_space=pltpu.VMEM),
         scratch_shapes=scratch,
         compiler_params=pltpu.CompilerParams(
-            collective_id=0, has_side_effects=True, vmem_limit_bytes=56 * 1024 * 1024
+            collective_id=0, has_side_effects=True, vmem_limit_bytes=44 * 1024 * 1024
         ),
         name="encoder",
     )(*operands)
+    spectrum = pl.pallas_call(
+        store,
+        out_shape=jax.ShapeDtypeStruct((OWN, 2, 2 * CH, 128), F32),
+        in_specs=[pl.BlockSpec(memory_space=pltpu.VMEM)],
+        out_specs=pl.BlockSpec(memory_space=pltpu.HBM),
+        scratch_shapes=[pltpu.SemaphoreType.DMA],
+        name="store",
+    )(spectrum)
     return spectrum.reshape(OWN, 2, CH, 2, 128)
 
 

time: 22.7 us -> 33.5 us (1.48)
  local copies, waits for them, and re-layouts: 1.57 us -> 9.77 us
  Pallas kernels: 21 us -> 23.2 us
    unnamed x1 -> x22, local copies, waits for them, and re-layouts: 1.57 us -> 9.77 us
    pallas_call x0 -> x1, Pallas kernels: none -> 1.57 us  [per_device(): pl.pallas_call(store, out_shape=jax.ShapeDtypeStruct((OWN, 2, 2 * CH, 128...]
    pallas_call x1, Pallas kernels: 21 us -> 21.7 us  [per_device(): pl.pallas_call(kernel, out_shape=jax.ShapeDtypeStruct((OWN, 2, 2 * CH, 12...]
where the time goes in v2:
time: 33.5 us; the launch traced here: 33 us
  Pallas kernels  23.2 us (69%)
  local copies, waits for them, and re-layouts  9.77 us (29%)
    pallas_call x1, Pallas kernels, per_device(): pl.pallas_call(kernel, out_shape=jax.ShapeDtypeStruct((OWN, 2, 2 * CH, 12...  21.7 us
    unnamed x22, local copies, waits for them, and re-layouts  9.77 us
    pallas_call x1, Pallas kernels, per_device(): pl.pallas_call(store, out_shape=jax.ShapeDtypeStruct((OWN, 2, 2 * CH, 128...  1.57 us

profile of v2, /device:TPU:1, one launch (start us, length us, event | category | flops | bytes accessed | tf_op | source)
XLA Modules:
  0.0 33.0 jit_solution(10378573571745522054)
XLA Ops:
  0.0 0.0 copy-start
  0.0 1.1 %copy-done = bf16[256,1536]{1,0:T(8,128)(2,1)S(1)} copy-done((bf16[256,1536]{1,0:T(8,128)(2,1)S(1)}, bf16[256,1536]{1,0:T(8,128)(2,1)}, u32[]{:S(2)}) %copy-start) | copy-done | bytes 786456
  1.1 0.0 copy-start.2
  1.1 1.0 %copy-done.2 = f32[4,256,128]{2,1,0:T(8,128)S(1)} copy-done((f32[4,256,128]{2,1,0:T(8,128)S(1)}, f32[4,256,128]{2,1,0:T(8,128)}, u32[]{:S(2)}) %copy-start.2) | copy-done | bytes 524312
  2.2 0.0 copy-start.3
  2.2 1.0 %copy-done.3 = bf16[16,8,1536]{2,1,0:T(8,128)(2,1)S(1)} copy-done((bf16[16,8,1536]{2,1,0:T(8,128)(2,1)S(1)}, bf16[16,8,1536]{2,1,0:T(8,128)(2,1)}, u32[]{:S(2)}) %copy-start.3) | copy-done | bytes 393240
  3.2 0.0 copy-start.4
  3.2 1.0 %copy-done.4 = bf16[128,1536]{1,0:T(8,128)(2,1)S(1)} copy-done((bf16[128,1536]{1,0:T(8,128)(2,1)S(1)}, bf16[128,1536]{1,0:T(8,128)(2,1)}, u32[]{:S(2)}) %copy-start.4) | copy-done | bytes 393240
  4.2 0.0 copy-start.5
  4.2 1.0 %copy-done.5 = bf16[128,1280]{1,0:T(8,128)(2,1)S(1)} copy-done((bf16[128,1280]{1,0:T(8,128)(2,1)S(1)}, bf16[128,1280]{1,0:T(8,128)(2,1)}, u32[]{:S(2)}) %copy-start.5) | copy-done | bytes 327704
  5.1 0.0 copy-start.6
  5.1 0.9 %copy-done.6 = bf16[16,16,5,5]{1,0,3,2:T(8,128)(2,1)S(1)} copy-done((bf16[16,16,5,5]{1,0,3,2:T(8,128)(2,1)S(1)}, bf16[16,16,5,5]{1,0,3,2:T(8,128)(2,1)}, u32[]{:S(2)}) %copy-start.6) | copy-done | bytes 12824
  6.0 0.0 copy-start.7
  6.0 0.9 %copy-done.7 = bf16[16,16,5,5]{1,0,3,2:T(8,128)(2,1)S(1)} copy-done((bf16[16,16,5,5]{1,0,3,2:T(8,128)(2,1)S(1)}, bf16[16,16,5,5]{1,0,3,2:T(8,128)(2,1)}, u32[]{:S(2)}) %copy-start.7) | copy-done | bytes 12824
  6.9 0.0 copy-start.8
  6.9 0.8 %copy-done.8 = bf16[256,128]{1,0:T(8,128)(2,1)S(1)} copy-done((bf16[256,128]{1,0:T(8,128)(2,1)S(1)}, bf16[256,128]{1,0:T(8,128)(2,1)}, u32[]{:S(2)}) %copy-start.8) | copy-done | bytes 65560
  7.8 0.0 copy-start.9
  7.8 0.7 %copy-done.9 = bf16[64,128]{1,0:T(8,128)(2,1)S(1)} copy-done((bf16[64,128]{1,0:T(8,128)(2,1)S(1)}, bf16[64,128]{1,0:T(8,128)(2,1)}, u32[]{:S(2)}) %copy-start.9) | copy-done | bytes 16408
  8.5 0.0 copy-start.10
  8.5 0.7 %copy-done.10 = f32[16]{0:T(128)S(1)} copy-done((f32[16]{0:T(128)S(1)}, f32[16]{0:T(128)}, u32[]{:S(2)}) %copy-start.10) | copy-done | bytes 88
  9.1 21.7 %encoder.1.source = f32[4,2,32,128]{3,2,1,0:T(8,128)S(1)} custom-call(bf16[128,1536]{1,0:T(8,128)(2,1)S(1)} %bitcast.5, bf16[5,5,16,16]{3,2,1,0:T(8,128)(2,1)S(1)} %bitcast.6, f32[1,16]{1,0:T(1,128)S(1)} %bitcast.8, bf16[5,5,16,16]{3,2,1,0:T(8,128)(2,1)S(1)} %bitcast.7, bf16[64,128]{1,0:T(8,128)(2,1)S(1)} %copy-done.9, bf16[128,1280]{1,0:T(8,128)(2,1)S(1)} %copy-done.5, ...), custom_call_target="tpu_custom_call" | custom-call | tf_op jit(solution)/shard_map/encoder/pallas_call | solution.py:428
  30.8 0.0 copy-start.1
  30.8 0.6 %copy-done.1 = f32[4,2,32,128]{3,2,1,0:T(8,128)} copy-done((f32[4,2,32,128]{3,2,1,0:T(8,128)}, f32[4,2,32,128]{3,2,1,0:T(8,128)S(1)}, u32[]{:S(2)}) %copy-start.1) | copy-done | bytes 131096
  31.5 1.6 %store.1 = f32[4,2,32,128]{3,2,1,0:T(8,128)} custom-call(f32[4,2,32,128]{3,2,1,0:T(8,128)} %copy-done.1), custom_call_target="tpu_custom_call" | custom-call | tf_op jit(solution)/shard_map/store/pallas_call | solution.py:439
Async XLA Ops:
  0.0 1.1 %copy-start = (bf16[256,1536]{1,0:T(8,128)(2,1)S(1)}, bf16[256,1536]{1,0:T(8,128)(2,1)}, u32[]{:S(2)}) copy-start(bf16[256,1536]{1,0:T(8,128)(2,1)} %constant.18.clone.fourier) | copy-start | bytes 2359300
  1.1 1.0 %copy-start.2 = (f32[4,256,128]{2,1,0:T(8,128)S(1)}, f32[4,256,128]{2,1,0:T(8,128)}, u32[]{:S(2)}) copy-start(f32[4,256,128]{2,1,0:T(8,128)} %constant.19.clone.phase) | copy-start | bytes 1572868
  2.2 1.0 %copy-start.3 = (bf16[16,8,1536]{2,1,0:T(8,128)(2,1)S(1)}, bf16[16,8,1536]{2,1,0:T(8,128)(2,1)}, u32[]{:S(2)}) copy-start(bf16[16,8,1536]{2,1,0:T(8,128)(2,1)} %param.11) | copy-start | bytes 1179652
  3.2 1.0 %copy-start.4 = (bf16[128,1536]{1,0:T(8,128)(2,1)S(1)}, bf16[128,1536]{1,0:T(8,128)(2,1)}, u32[]{:S(2)}) copy-start(bf16[128,1536]{1,0:T(8,128)(2,1)} %constant.16.clone.spread2) | copy-start | bytes 1179652
  4.2 1.0 %copy-start.5 = (bf16[128,1280]{1,0:T(8,128)(2,1)S(1)}, bf16[128,1280]{1,0:T(8,128)(2,1)}, u32[]{:S(2)}) copy-start(bf16[128,1280]{1,0:T(8,128)(2,1)} %constant.15.clone.spread1) | copy-start | bytes 983044
  5.1 0.9 %copy-start.6 = (bf16[16,16,5,5]{1,0,3,2:T(8,128)(2,1)S(1)}, bf16[16,16,5,5]{1,0,3,2:T(8,128)(2,1)}, u32[]{:S(2)}) copy-start(bf16[16,16,5,5]{1,0,3,2:T(8,128)(2,1)} %param.12) | copy-start | bytes 38404
  6.0 0.9 %copy-start.7 = (bf16[16,16,5,5]{1,0,3,2:T(8,128)(2,1)S(1)}, bf16[16,16,5,5]{1,0,3,2:T(8,128)(2,1)}, u32[]{:S(2)}) copy-start(bf16[16,16,5,5]{1,0,3,2:T(8,128)(2,1)} %param.14) | copy-start | bytes 38404
  6.9 0.8 %copy-start.8 = (bf16[256,128]{1,0:T(8,128)(2,1)S(1)}, bf16[256,128]{1,0:T(8,128)(2,1)}, u32[]{:S(2)}) copy-start(bf16[256,128]{1,0:T(8,128)(2,1)} %constant.17.clone.placed) | copy-start | bytes 196612
  7.8 0.7 %copy-start.9 = (bf16[64,128]{1,0:T(8,128)(2,1)S(1)}, bf16[64,128]{1,0:T(8,128)(2,1)}, u32[]{:S(2)}) copy-start(bf16[64,128]{1,0:T(8,128)(2,1)} %constant.14.clone.edge) | copy-start | bytes 49156
  8.5 0.7 %copy-start.10 = (f32[16]{0:T(128)S(1)}, f32[16]{0:T(128)}, u32[]{:S(2)}) copy-start(f32[16]{0:T(128)} %param.13) | copy-start | bytes 196
  30.8 0.6 %copy-start.1 = (f32[4,2,32,128]{3,2,1,0:T(8,128)}, f32[4,2,32,128]{3,2,1,0:T(8,128)S(1)}, u32[]{:S(2)}) copy-start(f32[4,2,32,128]{3,2,1,0:T(8,128)S(1)} %encoder.1.source) | copy-start | bytes 393220

commit v3 on v2

--- a/solution.py
+++ b/solution.py
@@ -427,19 +427,20 @@
     ]
     spectrum = pl.pallas_call(
         kernel,
-        out_shape=jax.ShapeDtypeStruct((OWN, 2, 2 * CH, 128), F32),
+        out_shape=pltpu.VMEM((OWN, 2, 2 * CH, 128), F32),
         in_specs=[pl.BlockSpec(memory_space=pltpu.HBM)] * len(operands),
         out_specs=pl.BlockSpec(memory_space=pltpu.VMEM),
         scratch_shapes=scratch,
         compiler_params=pltpu.CompilerParams(
-            collective_id=0, has_side_effects=True, vmem_limit_bytes=44 * 1024 * 1024
+            collective_id=0, has_side_effects=True, vmem_limit_bytes=56 * 1024 * 1024
         ),
         name="encoder",
     )(*operands)
     spectrum = pl.pallas_call(
         store,
         out_shape=jax.ShapeDtypeStruct((OWN, 2, 2 * CH, 128), F32),
-        in_specs=[pl.BlockSpec(memory_space=pltpu.VMEM)],
+        in_specs=[pl.BlockSpec(memory_space=pl.ANY)],
+        compiler_params=pltpu.CompilerParams(vmem_limit_bytes=1024 * 1024),
         out_specs=pl.BlockSpec(memory_space=pltpu.HBM),
         scratch_shapes=[pltpu.SemaphoreType.DMA],
         name="store",

time: 33.5 us -> 21.6 us (0.64); the launches traced: 33 us -> 21.5 us
  local copies, waits for them, and re-layouts: 9.77 us -> 0 us
  Pallas kernels: 23.2 us -> 21.5 us
    unnamed x22 -> x0, local copies, waits for them, and re-layouts: 9.77 us -> none
    pallas_call x1, Pallas kernels: 1.57 us -> 0.67 us  [per_device(): pl.pallas_call(store, out_shape=jax.ShapeDtypeStruct((OWN, 2, 2 * CH, 128...]
    pallas_call x1, Pallas kernels: 21.7 us -> 20.8 us  [per_device(): pl.pallas_call(kernel, out_shape=pltpu.VMEM((OWN, 2, 2 * CH, 128), F32),...]
where the time goes in v3:
time: 21.6 us; the launch traced here: 21.5 us
  Pallas kernels  21.5 us (100%)
    pallas_call x1, Pallas kernels, per_device(): pl.pallas_call(kernel, out_shape=pltpu.VMEM((OWN, 2, 2 * CH, 128), F32),...  20.8 us
    pallas_call x1, Pallas kernels, per_device(): pl.pallas_call(store, out_shape=jax.ShapeDtypeStruct((OWN, 2, 2 * CH, 128...  0.67 us

profile of v3, /device:TPU:1, one launch (start us, length us, event | category | flops | bytes accessed | tf_op | source)
XLA Modules:
  0.0 21.5 jit_solution(16093404624377555668)
XLA Ops:
  0.0 20.8 %encoder.1.source = f32[4,2,32,128]{3,2,1,0:T(8,128)S(1)} custom-call(bf16[128,1536]{1,0:T(8,128)(2,1)} %bitcast.5, bf16[5,5,16,16]{3,2,1,0:T(8,128)(2,1)} %bitcast.6, f32[1,16]{1,0:T(1,128)} %bitcast.8, bf16[5,5,16,16]{3,2,1,0:T(8,128)(2,1)} %bitcast.7, bf16[64,128]{1,0:T(8,128)(2,1)} %constant.14.clone.edge, bf16[128,1280]{1,0:T(8,128)(2,1)} %constant.15.clone.spread1, ...), custom_call_target="tpu_custom_call" | custom-call | tf_op jit(solution)/shard_map/encoder/pallas_call | solution.py:428
  20.8 0.7 %store.1 = f32[4,2,32,128]{3,2,1,0:T(8,128)} custom-call(f32[4,2,32,128]{3,2,1,0:T(8,128)S(1)} %encoder.1.source), custom_call_target="tpu_custom_call" | custom-call | tf_op jit(solution)/shard_map/store/pallas_call | solution.py:439

commit v4 on v3

--- a/solution.py
+++ b/solution.py
@@ -190,7 +190,7 @@
     atm, w1, bias, w2, edge, spread1, spread2, placed, fourier, phase, table, result,
     shifted, halo, w1_v, bias_v, w2_v, edge_v, spread1_v, spread2_v, fourier_v, phase_v, table_v,
     t1, t1h, t2, hsend, acc, hidden, mixed, packed, received,
-    load_sem, halo_send, halo_recv, a2a_send, a2a_recv,
+    load_sem, halo_send, halo_recv, a2a_send, a2a_recv, rows_in,
 ):
     me = lax.axis_index("lat")
     barrier = pltpu.get_barrier_semaphore()
@@ -216,19 +216,24 @@
         copy.start()
 
     others = peers(me)
-    for other in [lax.rem(me + 1, BANDS), lax.rem(me + BANDS - 1, BANDS)]:
+    column, depth = me % 8, me // 8
+    line = [8 * ((depth + k) % 4) + column for k in (1, 2, 3)]
+    row = [8 * depth + (column + k) % 8 for k in (1, 7, 2, 6, 3, 5, 4)]
+
+    def tell(semaphore, other):
         pl.semaphore_signal(
-            barrier, inc=1, device_id={"lat": other}, device_id_type=pl.DeviceIdType.MESH
+            semaphore, inc=1, device_id={"lat": other}, device_id_type=pl.DeviceIdType.MESH
         )
 
-    def greet(j, carry):
-        pl.semaphore_signal(
-            barrier, inc=1, device_id={"lat": lax.rem(me + j, BANDS)},
-            device_id_type=pl.DeviceIdType.MESH,
-        )
-        return carry
-
-    lax.fori_loop(2, BANDS - 1, greet, 0)
+    step = jnp.where(column == 7, 1, -1)
+    crossing = ((column == 7) & (me < BANDS - 1)) | ((column == 0) & (me > 0))
+
+    @pl.when(crossing)
+    def _():
+        tell(barrier, me + step)
+
+    for other in row + line:
+        tell(barrier, other)
 
     copies[0].wait()
     copies[1].wait()
@@ -236,7 +241,7 @@
         edge_v[...], shifted[256:384, :], preferred_element_type=F32
     ).astype(BF16)
 
-    pl.semaphore_wait(barrier, BANDS - 1)
+    pl.semaphore_wait(barrier, jnp.where(crossing, 11, 10))
 
     up = lax.max(me - 1, 0)
     down = lax.min(me + 1, BANDS - 1)
@@ -258,6 +263,9 @@
     @pl.when(me < BANDS - 1)
     def _():
         to_down.start()
+
+    for other in line:
+        tell(rows_in, other)
 
     copies[2].wait()
     copies[3].wait()
@@ -340,6 +348,7 @@
     far = swap_blocks(sums[:, :, 128:256])
     packed[...] = jnp.concatenate([near, far], axis=1).astype(BF16)
 
+    pl.semaphore_wait(rows_in, 3)
     for p in others:
         pltpu.make_async_remote_copy(
             src_ref=packed.at[p], dst_ref=received.at[me],
@@ -424,6 +433,7 @@
         pltpu.SemaphoreType.DMA((2,)),
         pltpu.SemaphoreType.DMA,
         pltpu.SemaphoreType.DMA,
+        pltpu.SemaphoreType.REGULAR,
     ]
     spectrum = pl.pallas_call(
         kernel,

time: 21.6 us -> 20.3 us (0.940)
  Pallas kernels: 21.5 us -> 20.2 us
    pallas_call x1, Pallas kernels: 20.8 us -> 19.5 us  [per_device(): pl.pallas_call(kernel, out_shape=pltpu.VMEM((OWN, 2, 2 * CH, 128), F32),...]
where the time goes in v4:
time: 20.3 us; the launch traced here: 20.2 us
  Pallas kernels  20.2 us (100%)
    pallas_call x1, Pallas kernels, per_device(): pl.pallas_call(kernel, out_shape=pltpu.VMEM((OWN, 2, 2 * CH, 128), F32),...  19.5 us
    pallas_call x1, Pallas kernels, per_device(): pl.pallas_call(store, out_shape=jax.ShapeDtypeStruct((OWN, 2, 2 * CH, 128...  0.67 us

profile of v4, /device:TPU:1, one launch (start us, length us, event | category | flops | bytes accessed | tf_op | source)
XLA Modules:
  0.0 20.2 jit_solution(11250870010697647952)
XLA Ops:
  0.0 19.5 %encoder.1.source = f32[4,2,32,128]{3,2,1,0:T(8,128)S(1)} custom-call(bf16[128,1536]{1,0:T(8,128)(2,1)} %bitcast.5, bf16[5,5,16,16]{3,2,1,0:T(8,128)(2,1)} %bitcast.6, f32[1,16]{1,0:T(1,128)} %bitcast.8, bf16[5,5,16,16]{3,2,1,0:T(8,128)(2,1)} %bitcast.7, bf16[64,128]{1,0:T(8,128)(2,1)} %constant.14.clone.edge, bf16[128,1280]{1,0:T(8,128)(2,1)} %constant.15.clone.spread1, ...), custom_call_target="tpu_custom_call" | custom-call | tf_op jit(solution)/shard_map/encoder/pallas_call | solution.py:438
  19.5 0.7 %store.1 = f32[4,2,32,128]{3,2,1,0:T(8,128)} custom-call(f32[4,2,32,128]{3,2,1,0:T(8,128)S(1)} %encoder.1.source), custom_call_target="tpu_custom_call" | custom-call | tf_op jit(solution)/shard_map/store/pallas_call | solution.py:449

commit v5 on v4

--- a/solution.py
+++ b/solution.py
@@ -212,9 +212,8 @@
         pltpu.make_async_copy(source, target, load_sem.at[n])
         for n, (source, target) in enumerate(loads)
     ]
-    for copy in copies:
-        copy.start()
-
+    copies[0].start()
+    copies[1].start()
     others = peers(me)
     column, depth = me % 8, me // 8
     line = [8 * ((depth + k) % 4) + column for k in (1, 2, 3)]
@@ -234,6 +233,9 @@
 
     for other in row + line:
         tell(barrier, other)
+
+    for copy in copies[2:]:
+        copy.start()
 
     copies[0].wait()
     copies[1].wait()
@@ -349,12 +351,17 @@
     packed[...] = jnp.concatenate([near, far], axis=1).astype(BF16)
 
     pl.semaphore_wait(rows_in, 3)
-    for p in others:
+
+    def send(p):
         pltpu.make_async_remote_copy(
             src_ref=packed.at[p], dst_ref=received.at[me],
             send_sem=a2a_send, recv_sem=a2a_recv,
             device_id={"lat": p}, device_id_type=pl.DeviceIdType.MESH,
         ).start()
+
+    pl.when(me != 1)(functools.partial(send, 1))
+    for p in others:
+        pl.when(p != 1)(functools.partial(send, p))
     received[me] = packed[me]
     copies[10].wait()
     some = pltpu.make_async_remote_copy(

time: 20.3 us -> 19.6 us (0.966)
  Pallas kernels: 20.2 us -> 19.4 us
    pallas_call x1, Pallas kernels: 19.5 us -> 18.8 us  [per_device(): pl.pallas_call(kernel, out_shape=pltpu.VMEM((OWN, 2, 2 * CH, 128), F32),...]
where the time goes in v5:
time: 19.6 us; the launch traced here: 19.4 us
  Pallas kernels  19.4 us (99%)
    pallas_call x1, Pallas kernels, per_device(): pl.pallas_call(kernel, out_shape=pltpu.VMEM((OWN, 2, 2 * CH, 128), F32),...  18.8 us
    pallas_call x1, Pallas kernels, per_device(): pl.pallas_call(store, out_shape=jax.ShapeDtypeStruct((OWN, 2, 2 * CH, 128...  0.67 us

profile of v5, /device:TPU:1, one launch (start us, length us, event | category | flops | bytes accessed | tf_op | source)
XLA Modules:
  0.0 19.4 jit_solution(16139529574720900612)
XLA Ops:
  0.0 18.8 %encoder.1.source = f32[4,2,32,128]{3,2,1,0:T(8,128)S(1)} custom-call(bf16[128,1536]{1,0:T(8,128)(2,1)} %bitcast.5, bf16[5,5,16,16]{3,2,1,0:T(8,128)(2,1)} %bitcast.6, f32[1,16]{1,0:T(1,128)} %bitcast.8, bf16[5,5,16,16]{3,2,1,0:T(8,128)(2,1)} %bitcast.7, bf16[64,128]{1,0:T(8,128)(2,1)} %constant.14.clone.edge, bf16[128,1280]{1,0:T(8,128)(2,1)} %constant.15.clone.spread1, ...), custom_call_target="tpu_custom_call" | custom-call | tf_op jit(solution)/shard_map/encoder/pallas_call | solution.py:445
  18.8 0.7 %store.1 = f32[4,2,32,128]{3,2,1,0:T(8,128)} custom-call(f32[4,2,32,128]{3,2,1,0:T(8,128)S(1)} %encoder.1.source), custom_call_target="tpu_custom_call" | custom-call | tf_op jit(solution)/shard_map/store/pallas_call | solution.py:456

commit v6 on v5

--- a/solution.py
+++ b/solution.py
@@ -28,7 +28,7 @@
     real = np.cos(phases) / math.sqrt(LON)
     imag = -np.sin(phases) / math.sqrt(LON)
     both = np.stack([real.reshape(BANDS, OWN, LON), imag.reshape(BANDS, OWN, LON)], axis=1)
-    return both.reshape(2 * ORDERS, LON).astype(BF16)
+    return both.reshape(2 * ORDERS, LON).T.astype(BF16)
 
 
 def phase_rows():
@@ -189,7 +189,7 @@
 def kernel(
     atm, w1, bias, w2, edge, spread1, spread2, placed, fourier, phase, table, result,
     shifted, halo, w1_v, bias_v, w2_v, edge_v, spread1_v, spread2_v, fourier_v, phase_v, table_v,
-    t1, t1h, t2, hsend, acc, hidden, mixed, packed, received,
+    t1, t1h, t2, t2n, hsend, acc, hidden, mixed, packed, received,
     load_sem, halo_send, halo_recv, a2a_send, a2a_recv, rows_in,
 ):
     me = lax.axis_index("lat")
@@ -212,9 +212,6 @@
         pltpu.make_async_copy(source, target, load_sem.at[n])
         for n, (source, target) in enumerate(loads)
     ]
-    copies[0].start()
-    copies[1].start()
-    others = peers(me)
     column, depth = me % 8, me // 8
     line = [8 * ((depth + k) % 4) + column for k in (1, 2, 3)]
     row = [8 * depth + (column + k) % 8 for k in (1, 7, 2, 6, 3, 5, 4)]
@@ -227,11 +224,16 @@
     step = jnp.where(column == 7, 1, -1)
     crossing = ((column == 7) & (me < BANDS - 1)) | ((column == 0) & (me > 0))
 
+    for other in row[:2]:
+        tell(barrier, other)
+
     @pl.when(crossing)
     def _():
         tell(barrier, me + step)
 
-    for other in row + line:
+    copies[0].start()
+    copies[1].start()
+    for other in row[2:] + line:
         tell(barrier, other)
 
     for copy in copies[2:]:
@@ -307,7 +309,12 @@
             ]
     t2[160:224, 0:640] = jnp.zeros((64, 640), BF16)
     copies[7].wait()
-    mixed[:, 640:768] = nt(fourier_v[...], shifted[256:384, :]).astype(BF16)
+    mixed[:, 640:768] = jnp.dot(
+        shifted[256:384, :], fourier_v[...], preferred_element_type=F32
+    ).T.astype(BF16)
+
+    copies[8].wait()
+    t2n[...] = t2[...].astype(F32).T.astype(BF16)
 
     @pl.when(me > 0)
     def _():
@@ -334,7 +341,7 @@
     hidden[0:32, :] = gelu(acc[0:32, :] + more[0:32]).astype(BF16)
     hidden[96:128, :] = gelu(acc[96:128, :] + more[32:64]).astype(BF16)
 
-    spectra = nt(fourier_v[...], hidden[...])
+    spectra = jnp.dot(hidden[...], fourier_v[...], preferred_element_type=F32).T
     swapped = pltpu.roll(spectra.reshape(BANDS, 8, 128), 4, 1).reshape(256, 128)
     copies[9].wait()
     mixed[:, 256:384] = spectra.astype(BF16)
@@ -344,13 +351,14 @@
         mixed[:, 128 * high : 128 * high + 128] = (straight + crossed).astype(BF16)
         mixed[:, 128 * low : 128 * low + 128] = (straight - crossed).astype(BF16)
 
-    copies[8].wait()
-    sums = nt(mixed[...], t2[...]).reshape(BANDS, 8, 256)
+    sums = jnp.dot(mixed[...], t2n[...], preferred_element_type=F32).reshape(BANDS, 8, 256)
     near = swap_blocks(sums[:, :, 0:128])
     far = swap_blocks(sums[:, :, 128:256])
     packed[...] = jnp.concatenate([near, far], axis=1).astype(BF16)
 
     pl.semaphore_wait(rows_in, 3)
+
+    others = peers(me)
 
     def send(p):
         pltpu.make_async_remote_copy(
@@ -429,6 +437,7 @@
         pltpu.VMEM((128, 640), BF16),
         pltpu.VMEM((64, 320), BF16),
         pltpu.VMEM((256, 768), BF16),
+        pltpu.VMEM((768, 256), BF16),
         pltpu.VMEM((64, LON), BF16),
         pltpu.VMEM((128, LON), F32),
         pltpu.VMEM((128, LON), BF16),

time: 19.6 us -> 19.4 us (0.990)
  no operation moved by 1% of the time
where the time goes in v6:
time: 19.4 us; the launch traced here: 19.3 us
  Pallas kernels  19.3 us (99%)
    pallas_call x1, Pallas kernels, per_device(): pl.pallas_call(kernel, out_shape=pltpu.VMEM((OWN, 2, 2 * CH, 128), F32),...  18.6 us
    pallas_call x1, Pallas kernels, per_device(): pl.pallas_call(store, out_shape=jax.ShapeDtypeStruct((OWN, 2, 2 * CH, 128...  0.67 us

profile of v6, /device:TPU:1, one launch (start us, length us, event | category | flops | bytes accessed | tf_op | source)
XLA Modules:
  0.0 19.3 jit_solution(3765863652612868383)
XLA Ops:
  0.0 18.6 %encoder.1.source = f32[4,2,32,128]{3,2,1,0:T(8,128)S(1)} custom-call(bf16[128,1536]{1,0:T(8,128)(2,1)} %bitcast.5, bf16[5,5,16,16]{3,2,1,0:T(8,128)(2,1)} %bitcast.6, f32[1,16]{1,0:T(1,128)} %bitcast.8, bf16[5,5,16,16]{3,2,1,0:T(8,128)(2,1)} %bitcast.7, bf16[64,128]{1,0:T(8,128)(2,1)} %constant.14.clone.edge, bf16[128,1280]{1,0:T(8,128)(2,1)} %constant.15.clone.spread1, ...), custom_call_target="tpu_custom_call" | custom-call | tf_op jit(solution)/shard_map/encoder/pallas_call | solution.py:454
  18.6 0.7 %store.1 = f32[4,2,32,128]{3,2,1,0:T(8,128)} custom-call(f32[4,2,32,128]{3,2,1,0:T(8,128)S(1)} %encoder.1.source), custom_call_target="tpu_custom_call" | custom-call | tf_op jit(solution)/shard_map/store/pallas_call | solution.py:465

commit v7 on v6

--- a/solution.py
+++ b/solution.py
@@ -250,12 +250,12 @@
     up = lax.max(me - 1, 0)
     down = lax.min(me + 1, BANDS - 1)
     to_up = pltpu.make_async_remote_copy(
-        src_ref=hsend.at[pl.ds(0, 32), :], dst_ref=halo.at[pl.ds(160, 32), :],
+        src_ref=hsend.at[pl.ds(0, 32), :], dst_ref=halo.at[1, pl.ds(64, 32), :],
         send_sem=halo_send.at[0], recv_sem=halo_recv.at[0],
         device_id={"lat": up}, device_id_type=pl.DeviceIdType.MESH,
     )
     to_down = pltpu.make_async_remote_copy(
-        src_ref=hsend.at[pl.ds(32, 32), :], dst_ref=halo.at[pl.ds(128, 32), :],
+        src_ref=hsend.at[pl.ds(32, 32), :], dst_ref=halo.at[0, pl.ds(64, 32), :],
         send_sem=halo_send.at[1], recv_sem=halo_recv.at[1],
         device_id={"lat": down}, device_id_type=pl.DeviceIdType.MESH,
     )
@@ -280,8 +280,10 @@
                 16 * dx : 16 * dx + 16, 128 * y : 128 * y + 128
             ]
         for e in range(4):
-            t1h[16 * e : 16 * e + 16, 64 * dx : 64 * dx + 64] = res1[
-                16 * dx : 16 * dx + 16, 1024 + 64 * e : 1088 + 64 * e
+            side, at = e // 2, 16 * (e % 2)
+            start = 1024 + 64 * e + 32 * side
+            t1h[side, at : at + 16, 32 * dx : 32 * dx + 32] = res1[
+                16 * dx : 16 * dx + 16, start : start + 32
             ]
 
     own = shifted[256:384, :].astype(F32)
@@ -316,30 +318,29 @@
     copies[8].wait()
     t2n[...] = t2[...].astype(F32).T.astype(BF16)
 
-    @pl.when(me > 0)
-    def _():
-        to_up.wait_send()
-        to_down.wait_recv()
-
-    @pl.when(me < BANDS - 1)
-    def _():
-        to_down.wait_send()
-        to_up.wait_recv()
-
     @pl.when(me == 0)
     def _():
-        halo[128:160, :] = jnp.zeros((32, LON), BF16)
+        halo[0, 64:96, :] = jnp.zeros((32, LON), BF16)
 
     @pl.when(me == BANDS - 1)
     def _():
-        halo[160:192, :] = jnp.zeros((32, LON), BF16)
-
-    rim = halo[128:192, :].astype(F32)
-    for dx in (0, 1, 3, 4):
-        halo[64 * dx : 64 * dx + 64, :] = pltpu.roll(rim, (2 - dx) % LON, 1).astype(BF16)
-    more = jnp.dot(t1h[...], halo[...], preferred_element_type=F32)
-    hidden[0:32, :] = gelu(acc[0:32, :] + more[0:32]).astype(BF16)
-    hidden[96:128, :] = gelu(acc[96:128, :] + more[32:64]).astype(BF16)
+        halo[1, 64:96, :] = jnp.zeros((32, LON), BF16)
+
+    def edge_of(side):
+        rim = halo[side, 64:96, :].astype(F32)
+        for dx in (0, 1, 3, 4):
+            halo[side, 32 * dx : 32 * dx + 32, :] = pltpu.roll(rim, (2 - dx) % LON, 1).astype(BF16)
+        more = jnp.dot(t1h[side], halo[side], preferred_element_type=F32)
+        rows = pl.ds(pl.multiple_of(96 * side, 32), 32)
+        hidden[rows, :] = gelu(acc[rows, :] + more).astype(BF16)
+
+    core = me % 2
+    pl.when(core == 0)(to_up.wait_recv)
+    pl.when(core == 1)(to_down.wait_recv)
+    edge_of(1 - core)
+    pl.when((core == 0) & (me > 0))(to_down.wait_recv)
+    pl.when((core == 1) & (me < BANDS - 1))(to_up.wait_recv)
+    edge_of(core)
 
     spectra = jnp.dot(hidden[...], fourier_v[...], preferred_element_type=F32).T
     swapped = pltpu.roll(spectra.reshape(BANDS, 8, 128), 4, 1).reshape(256, 128)
@@ -397,6 +398,8 @@
                     16 * a : 16 * a + 16, 128 * q : 128 * q + 128
                 ]
     some.wait_send()
+    pl.when(me > 0)(to_up.wait_send)
+    pl.when(me < BANDS - 1)(to_down.wait_send)
 
 
 def store(source, target, semaphore):
@@ -424,7 +427,7 @@
     )
     scratch = [
         pltpu.VMEM((640, LON), BF16),
-        pltpu.VMEM((320, LON), BF16),
+        pltpu.VMEM((2, 160, LON), BF16),
         pltpu.VMEM((5, 5, CH, CH), BF16),
         pltpu.VMEM((1, CH), F32),
         pltpu.VMEM((5, 5, CH, CH), BF16),
@@ -435,7 +438,7 @@
         pltpu.VMEM(phase.shape, F32),
         pltpu.VMEM(table.shape[1:], BF16),
         pltpu.VMEM((128, 640), BF16),
-        pltpu.VMEM((64, 320), BF16),
+        pltpu.VMEM((2, 32, 160), BF16),
         pltpu.VMEM((256, 768), BF16),
         pltpu.VMEM((768, 256), BF16),
         pltpu.VMEM((64, LON), BF16),

time: 19.4 us -> 19.2 us (0.990)
  Pallas kernels: 19.3 us -> 19.1 us
where the time goes in v7:
time: 19.2 us; the launch traced here: 19.1 us
  Pallas kernels  19.1 us (99%)
    pallas_call x1, Pallas kernels, per_device(): pl.pallas_call(kernel, out_shape=pltpu.VMEM((OWN, 2, 2 * CH, 128), F32),...  18.4 us
    pallas_call x1, Pallas kernels, per_device(): pl.pallas_call(store, out_shape=jax.ShapeDtypeStruct((OWN, 2, 2 * CH, 128...  0.67 us

profile of v7, /device:TPU:1, one launch (start us, length us, event | category | flops | bytes accessed | tf_op | source)
XLA Modules:
  0.0 19.1 jit_solution(3744363648057512770)
XLA Ops:
  0.0 18.4 %encoder.1.source = f32[4,2,32,128]{3,2,1,0:T(8,128)S(1)} custom-call(bf16[128,1536]{1,0:T(8,128)(2,1)} %bitcast.5, bf16[5,5,16,16]{3,2,1,0:T(8,128)(2,1)} %bitcast.6, f32[1,16]{1,0:T(1,128)} %bitcast.8, bf16[5,5,16,16]{3,2,1,0:T(8,128)(2,1)} %bitcast.7, bf16[64,128]{1,0:T(8,128)(2,1)} %constant.14.clone.edge, bf16[128,1280]{1,0:T(8,128)(2,1)} %constant.15.clone.spread1, ...), custom_call_target="tpu_custom_call" | custom-call | tf_op jit(solution)/shard_map/encoder/pallas_call | solution.py:457
  18.4 0.7 %store.1 = f32[4,2,32,128]{3,2,1,0:T(8,128)} custom-call(f32[4,2,32,128]{3,2,1,0:T(8,128)S(1)} %encoder.1.source), custom_call_target="tpu_custom_call" | custom-call | tf_op jit(solution)/shard_map/store/pallas_call | solution.py:468

commit v8 on v7

--- a/solution.py
+++ b/solution.py
@@ -343,22 +343,9 @@
     edge_of(core)
 
     spectra = jnp.dot(hidden[...], fourier_v[...], preferred_element_type=F32).T
-    swapped = pltpu.roll(spectra.reshape(BANDS, 8, 128), 4, 1).reshape(256, 128)
+    whole, crossing_parts = spectra, pltpu.roll(spectra.reshape(BANDS, 8, 128), 4, 1)
+    crossing_parts = crossing_parts.reshape(256, 128)
     copies[9].wait()
-    mixed[:, 256:384] = spectra.astype(BF16)
-    for step, low, high in ((1, 1, 3), (2, 0, 4)):
-        straight = phase_v[2 * step - 2] * spectra
-        crossed = phase_v[2 * step - 1] * swapped
-        mixed[:, 128 * high : 128 * high + 128] = (straight + crossed).astype(BF16)
-        mixed[:, 128 * low : 128 * low + 128] = (straight - crossed).astype(BF16)
-
-    sums = jnp.dot(mixed[...], t2n[...], preferred_element_type=F32).reshape(BANDS, 8, 256)
-    near = swap_blocks(sums[:, :, 0:128])
-    far = swap_blocks(sums[:, :, 128:256])
-    packed[...] = jnp.concatenate([near, far], axis=1).astype(BF16)
-
-    pl.semaphore_wait(rows_in, 3)
-
     others = peers(me)
 
     def send(p):
@@ -368,9 +355,26 @@
             device_id={"lat": p}, device_id_type=pl.DeviceIdType.MESH,
         ).start()
 
-    pl.when(me != 1)(functools.partial(send, 1))
-    for p in others:
-        pl.when(p != 1)(functools.partial(send, p))
+    for low, high in ((0, 8), (8, BANDS)):
+        rows = slice(8 * low, 8 * high)
+        spectra, swapped = whole[rows], crossing_parts[rows]
+        mixed[rows, 256:384] = spectra.astype(BF16)
+        for shift, less, more in ((1, 1, 3), (2, 0, 4)):
+            straight = phase_v[2 * shift - 2, rows, :] * spectra
+            crossed = phase_v[2 * shift - 1, rows, :] * swapped
+            mixed[rows, 128 * more : 128 * more + 128] = (straight + crossed).astype(BF16)
+            mixed[rows, 128 * less : 128 * less + 128] = (straight - crossed).astype(BF16)
+        sums = jnp.dot(mixed[rows, :], t2n[...], preferred_element_type=F32)
+        sums = sums.reshape(high - low, 8, 256)
+        near = swap_blocks(sums[:, :, 0:128])
+        far = swap_blocks(sums[:, :, 128:256])
+        packed[low:high] = jnp.concatenate([near, far], axis=1).astype(BF16)
+        if low == 0:
+            pl.semaphore_wait(rows_in, 3)
+            pl.when(me != 1)(functools.partial(send, 1))
+        for p in others:
+            pl.when((p != 1) & (p >= low) & (p < high))(functools.partial(send, p))
+
     received[me] = packed[me]
     copies[10].wait()
     some = pltpu.make_async_remote_copy(

time: 19.2 us -> 19.1 us (level)
  no operation moved by 1% of the time
where the time goes in v8:
time: 19.1 us; the launch traced here: 19 us
  Pallas kernels  19 us (99%)
    pallas_call x1, Pallas kernels, per_device(): pl.pallas_call(kernel, out_shape=pltpu.VMEM((OWN, 2, 2 * CH, 128), F32),...  18.4 us
    pallas_call x1, Pallas kernels, per_device(): pl.pallas_call(store, out_shape=jax.ShapeDtypeStruct((OWN, 2, 2 * CH, 128...  0.67 us

profile of v8, /device:TPU:1, one launch (start us, length us, event | category | flops | bytes accessed | tf_op | source)
XLA Modules:
  0.0 19.0 jit_solution(7436619227441836233)
XLA Ops:
  0.0 18.4 %encoder.1.source = f32[4,2,32,128]{3,2,1,0:T(8,128)S(1)} custom-call(bf16[128,1536]{1,0:T(8,128)(2,1)} %bitcast.5, bf16[5,5,16,16]{3,2,1,0:T(8,128)(2,1)} %bitcast.6, f32[1,16]{1,0:T(1,128)} %bitcast.8, bf16[5,5,16,16]{3,2,1,0:T(8,128)(2,1)} %bitcast.7, bf16[64,128]{1,0:T(8,128)(2,1)} %constant.14.clone.edge, bf16[128,1280]{1,0:T(8,128)(2,1)} %constant.15.clone.spread1, ...), custom_call_target="tpu_custom_call" | custom-call | tf_op jit(solution)/shard_map/encoder/pallas_call | solution.py:461
  18.4 0.7 %store.1 = f32[4,2,32,128]{3,2,1,0:T(8,128)} custom-call(f32[4,2,32,128]{3,2,1,0:T(8,128)S(1)} %encoder.1.source), custom_call_target="tpu_custom_call" | custom-call | tf_op jit(solution)/shard_map/store/pallas_call | solution.py:472
